TPU v7x, 32 devices: a whole 2x2x4 slice. The times are simulated.
32 devices in a mesh: groups: 2 (over y), fsdp: 4 (over z), tensor: 2 (over core), adapter: 2 (over x).
Axes of the slice: x: 2, y: 2, z: 4, core: 2. Of those that a mesh axis runs over, the one named last changes fastest.
Arguments:
- acts: bfloat16 [8192, 5120], P(('groups', 'fsdp'), ('adapter', 'tensor')), parts along dimension 0, may hold values from -6 to 6
- cotangent: bfloat16 [8192, 2, 1024], P(('groups', 'fsdp', 'adapter'), None, 'tensor'), parts along dimension 0, may hold values from -1.5 to 1.5
- key_value_weight: bfloat16 [5120, 2, 1024], P(('adapter', 'fsdp'), None, 'tensor'), may hold values from -0.078125 to 0.078125
- adapter_first_factor: bfloat16 [96, 2, 327680], P(None, None, ('adapter', 'tensor', 'fsdp')), may hold values from -0.078125 to 0.078125
- adapter_second_factor: bfloat16 [96, 2, 64, 1024], P(None, None, 'fsdp', 'tensor'), may hold values from -0.75 to 0.75
- adapter_of_block: int32 [32], P('groups'), parts along dimension 0, may hold values from 0 to 95
- occupied_rows: int32 [32], P('groups'), parts along dimension 0, may hold values from 32 to 256, as said below
Outputs:
- input_gradient: bfloat16 [8192, 5120], P(('groups', 'fsdp'), ('adapter', 'tensor')), parts along dimension 0
- down_grad: bfloat16 [192, 2, 327680], P('groups', None, ('adapter', 'tensor', 'fsdp')), parts along dimension 0
- up_grad: bfloat16 [192, 2, 64, 1024], P('groups', None, 'fsdp', 'tensor'), parts along dimension 0
There are 2 independent parts, one for each index of `groups`. A program takes and returns all parts, laid end to end along the dimension named above; an argument that names none is the same for every part. Nothing has to cross between parts.
Inputs may be any that keep to these rules, and one draw needn't show every extreme that they name: The first occupied_rows rows of a block hold tokens, the rest is padding; in every draw some block is full.
All inputs are finite; a program needn't handle non-finite values.
Results may differ from a plain program's by a relative error of at most 0.014.
Values may be sent and summed in bfloat16 or wider, within the bound.
A program may use at most 128 MiB of HBM per device.

v0:
```python
import jax
import jax.numpy as jnp
from jax import lax
from jax.sharding import PartitionSpec as P

ADAPTER_TOTAL = 96
ADAPTER_RANK = 64
BLOCK = 256


adapter_scale = 2.0


def on_device(
    acts,
    cotangent,
    key_value_weight,
    adapter_first_factor,
    adapter_second_factor,
    adapter_of_block,
    occupied_rows,
):
    fsdp_count = lax.axis_size("fsdp")
    fsdp_index = lax.axis_index("fsdp")
    adapter_index = lax.axis_index("adapter")
    count_of_rows = acts.shape[0]
    feature_columns = acts.shape[1]
    block_count = count_of_rows // BLOCK
    quarter_rows = cotangent.shape[0]
    head_half = cotangent.shape[2]
    portion_length = adapter_first_factor.shape[2]
    rank_portion = adapter_second_factor.shape[2]
    live_mine = lax.dynamic_slice_in_dim(occupied_rows, fsdp_index * block_count, block_count, 0)
    limits = jnp.repeat(live_mine, BLOCK, total_repeat_length=count_of_rows)
    limit_quarter = lax.dynamic_slice_in_dim(limits, adapter_index * quarter_rows, quarter_rows, 0)
    offsets = adapter_index * quarter_rows + jnp.arange(quarter_rows, dtype=jnp.int32)
    kept_rows = offsets % BLOCK < limit_quarter
    masked = jnp.where(kept_rows[:, None, None], cotangent, jnp.zeros_like(cotangent))
    cot_full = lax.all_gather(masked, "adapter", axis=0, tiled=True)
    departing_down = jnp.take(adapter_first_factor, adapter_of_block, axis=0)
    departing_up = jnp.take(adapter_second_factor, adapter_of_block, axis=0)
    fetched_down, fetched_up = (
        lax.all_to_all(departing_down, "fsdp", split_axis=0, concat_axis=0, tiled=True),
        lax.all_to_all(departing_up, "fsdp", split_axis=0, concat_axis=0, tiled=True),
    )
    own_down = fetched_down.reshape(fsdp_count, block_count, 2, portion_length).transpose(
        1, 2, 0, 3
    )
    own_down = own_down.reshape(block_count, 2, feature_columns, ADAPTER_RANK)
    own_up = fetched_up.reshape(fsdp_count, block_count, 2, rank_portion, head_half).transpose(
        1, 2, 0, 3, 4
    )
    own_up = own_up.reshape(block_count, 2, ADAPTER_RANK, head_half)
    cotangent_blocks = cot_full.reshape(block_count, BLOCK, 2, head_half)
    activation_blocks = acts.reshape(block_count, BLOCK, feature_columns)
    feature_part = jnp.einsum(
        "bnd,bcdr->bncr", activation_blocks, own_down, preferred_element_type=jnp.float32
    )
    head_part = jnp.einsum(
        "bnch,bcrh->bncr", cotangent_blocks, own_up, preferred_element_type=jnp.float32
    )
    head_total = lax.psum(head_part.astype(jnp.bfloat16), "tensor")
    feature_total = lax.psum(feature_part.astype(jnp.bfloat16), ("tensor", "adapter"))
    adapter_term = adapter_scale * jnp.einsum(
        "oyet,oemt->oym", head_total, own_down, preferred_element_type=jnp.float32
    )
    adapter_term = adapter_term.reshape(count_of_rows, feature_columns)
    block_down_factor = adapter_scale * jnp.einsum(
        "mky,mkzl->mzyl", activation_blocks, head_total, preferred_element_type=jnp.float32
    )
    block_up_factor = adapter_scale * jnp.einsum(
        "ijfm,ijfy->ifmy", feature_total, cotangent_blocks, preferred_element_type=jnp.float32
    )
    partial_value = jnp.einsum(
        "nch,dch->nd",
        cot_full,
        lax.all_gather(key_value_weight, "fsdp", axis=0, tiled=True),
        preferred_element_type=jnp.float32,
    )
    frozen_path_gradient = lax.psum_scatter(
        partial_value.astype(jnp.bfloat16), "tensor", scatter_dimension=1, tiled=True
    ).astype(jnp.float32)
    input_gradient = (frozen_path_gradient + adapter_term).astype(jnp.bfloat16)
    send_down = block_down_factor.reshape(block_count, 2, fsdp_count, portion_length).transpose(
        2, 0, 1, 3
    )
    send_down = send_down.reshape(fsdp_count * block_count, 2, portion_length)
    send_up = block_up_factor.reshape(
        block_count, 2, fsdp_count, rank_portion, head_half
    ).transpose(2, 0, 1, 3, 4)
    send_up = send_up.reshape(fsdp_count * block_count, 2, rank_portion, head_half)
    back_down, back_up = (
        lax.all_to_all(
            send_down.astype(jnp.bfloat16), "fsdp", split_axis=0, concat_axis=0, tiled=True
        ).astype(send_down.dtype),
        lax.all_to_all(
            send_up.astype(jnp.bfloat16), "fsdp", split_axis=0, concat_axis=0, tiled=True
        ).astype(send_up.dtype),
    )
    selector = (
        adapter_of_block[None, :] == jnp.arange(ADAPTER_TOTAL, dtype=jnp.int32)[:, None]
    ).astype(jnp.float32)
    down_factor_table = jnp.dot(
        selector, back_down.reshape(back_down.shape[0], -1), precision=lax.Precision.HIGHEST
    )
    table_up = jnp.dot(
        selector, back_up.reshape(back_up.shape[0], -1), precision=lax.Precision.HIGHEST
    )
    down_grad = down_factor_table.reshape(ADAPTER_TOTAL, 2, portion_length).astype(jnp.bfloat16)
    up_grad = table_up.reshape(ADAPTER_TOTAL, 2, rank_portion, head_half).astype(jnp.bfloat16)
    return (input_gradient, down_grad, up_grad)


def solution(mesh):
    in_specs = (
        P(("groups", "fsdp"), ("adapter", "tensor")),
        P(("groups", "fsdp", "adapter"), None, "tensor"),
        P(("adapter", "fsdp"), None, "tensor"),
        P(None, None, ("adapter", "tensor", "fsdp")),
        P(None, None, "fsdp", "tensor"),
        P("groups"),
        P("groups"),
    )
    out_specs = (
        P(("groups", "fsdp"), ("adapter", "tensor")),
        P("groups", None, ("adapter", "tensor", "fsdp")),
        P("groups", None, "fsdp", "tensor"),
    )
    return jax.shard_map(
        on_device, mesh=mesh, in_specs=in_specs, out_specs=out_specs, check_vma=False
    )
```

profile of v0, /device:TPU:0, one launch (start us, length us, event | category | flops | bytes accessed | tf_op | source)
XLA Modules:
  0.0 279.0 jit_solution(3011775757280563480)
XLA Ops:
  8.0 0.0 copy-start
  8.0 0.0 all-gather.3.cloned.1.call-start
  8.1 0.9 dynamic_slice.6
  8.9 0.6 fusion.31
  9.5 3.2 %select_select_fusion = s32[1024]{0:T(1024)S(1)} fusion(pred[1024]{0:T(1024)(128)(4,1)} %constant.167, pred[1024]{0:T(1024)(128)(4,1)} %constant.168, pred[1024]{0:T(1024)(128)(4,1)} %constant.169, s32[]{:T(128)} %bitcast.3, s32[]{:T(128)} %bitcast, s32[]{:T(128)} %bitcast.1, s32[]{:T(128)} %bitcast.2), kind=kLoop, calls=%fused_computation.32 | loop fusion | flops 3072 | bytes 7184 | tf_op jit(solution)/shard_map/jit(_take)/gather | solution.py:34
  12.8 0.1 fusion.30
  12.8 2.4 copy_select_fusion
  15.2 0.0 copy-start.4
  15.2 0.0 all-gather.3.cloned.1.call-update
  15.2 0.0 all-gather.5.cloned.1.call-start
  15.3 2.6 copy.18
  17.9 0.0 all-gather.5.cloned.1.call-update
  17.9 0.0 copy-done.4
  17.9 0.0 copy-done
  17.9 1.4 gather_fusion
  19.3 1.9 broadcast_select_fusion.1
  21.3 6.3 %all-to-all-start = ((bf16[16,2,16,512]{3,2,1,0:T(8,128)(2,1)}), bf16[16,2,16,512]{3,2,1,0:T(8,128)(2,1)S(1)}, u32[]{:S(2)}, u32[]{:S(2)}) async-start(bf16[16,2,16,512]{3,2,1,0:T(8,128)(2,1)} %broadcast_select_fusion.1), calls=%async_computation.1 | async-start | bytes 1048576 | tf_op jit(solution)/shard_map/all_to_all | solution.py:44
  27.6 6.4 %gather_fusion.1 = bf16[16,2,20480]{2,1,0:T(2,128)(2,1)S(1)} fusion(bf16[96,2,20480]{2,1,0:T(2,128)(2,1)} %param.12, s32[1024]{0:T(1024)S(1)} %pad_clamp_fusion), kind=kCustom, calls=%fused_computation.1 | custom fusion | bytes 2621504 | tf_op jit(solution)/shard_map/jit(_take)/gather | solution.py:40
  34.0 2.3 broadcast_select_fusion
  36.3 5.8 %all-to-all-done = bf16[16,2,16,512]{3,2,1,0:T(8,128)(2,1)S(1)} async-done(((bf16[16,2,16,512]{3,2,1,0:T(8,128)(2,1)}), bf16[16,2,16,512]{3,2,1,0:T(8,128)(2,1)S(1)}, u32[]{:S(2)}, u32[]{:S(2)}) %all-to-all-start) | async-done | bytes 524320 | tf_op jit(solution)/shard_map/all_to_all | solution.py:44
  42.1 3.5 %all-to-all-start.1 = ((bf16[16,2,20480]{2,1,0:T(2,128)(2,1)}), bf16[16,2,20480]{2,1,0:T(2,128)(2,1)S(1)}, u32[]{:S(2)}, u32[]{:S(2)}) async-start(bf16[16,2,20480]{2,1,0:T(2,128)(2,1)} %broadcast_select_fusion), calls=%async_computation.2 | async-start | bytes 2621440 | tf_op jit(solution)/shard_map/all_to_all | solution.py:43
  45.6 0.0 all-reduce.5.cloned.1.call-start
  45.7 51.9 %all-to-all-done.1 = bf16[16,2,20480]{2,1,0:T(2,128)(2,1)S(1)} async-done(((bf16[16,2,20480]{2,1,0:T(2,128)(2,1)}), bf16[16,2,20480]{2,1,0:T(2,128)(2,1)S(1)}, u32[]{:S(2)}, u32[]{:S(2)}) %all-to-all-start.1) | async-done | bytes 1310752 | tf_op jit(solution)/shard_map/all_to_all | solution.py:43
  97.6 2.1 copy.62
  99.7 3.6 %reshape.128 = bf16[4,2,1280,64]{3,2,1,0:T(8,128)(2,1)S(1)} reshape(bf16[4,2,4,20480]{3,2,1,0:T(4,128)(2,1)} %bitcast.85) | data formatting | bytes 2621440 | tf_op jit(solution)/shard_map/reshape | solution.py:49
  103.3 3.4 %fusion.18 = bf16[4,256,2,64]{1,3,2,0:T(8,128)(2,1)} fusion(bf16[4,2,1280,64]{3,2,1,0:T(8,128)(2,1)S(1)} %reshape.128, bf16[4,256,1280,1]{2,1,3,0:T(8,128)(2,1)} %bitcast.81), kind=kOutput, calls=%fused_computation.23 | convolution fusion | flops 335675392 | bytes 4194304 | tf_op jit(solution)/shard_map/bnd,bcdr->bncr/dot_general | solution.py:56
  106.7 0.0 all-reduce.5.cloned.1.call-update
  106.7 0.0 all-reduce.3.cloned.1.call-start
  106.8 0.0 all-gather.3.cloned.1.call-done
  106.8 3.1 %fusion.19 = bf16[4,256,2,64]{1,3,2,0:T(8,128)(2,1)} fusion(bf16[4,2,64,512]{3,2,1,0:T(8,128)(2,1)S(1)} %bitcast.89, bf16[4,256,2,512]{3,1,0,2:T(8,128)(2,1)} %bitcast.91), kind=kOutput, calls=%fused_computation.24 | convolution fusion | flops 134348800 | bytes 2883584 | tf_op jit(solution)/shard_map/bnch,bcrh->bncr/dot_general | solution.py:59
  109.9 0.0 all-reduce.3.cloned.1.call-update
  109.9 0.0 reduce-scatter.2.cloned.1.call-start
  109.9 51.5 %all-gather.5.cloned.1.call-done = bf16[2560,2,512]{2,0,1:T(8,128)(2,1)} async-done(((bf16[640,2,512]{2,0,1:T(8,128)(2,1)}), bf16[2560,2,512]{2,0,1:T(8,128)(2,1)}) %all-gather.5.cloned.1.call-update) | async-done | bytes 5242896 | tf_op jit(solution)/shard_map/all_gather | solution.py:77
  161.4 10.3 %bitcast_convert_fusion = bf16[1024,2560]{1,0:T(8,128)(2,1)} fusion(bf16[1024,2,512]{2,0,1:T(8,128)(2,1)} %all-gather.3.cloned.1.call-done, bf16[2560,2,512]{2,0,1:T(8,128)(2,1)} %all-gather.5.cloned.1.call-done), kind=kOutput, calls=%fused_computation.3 | convolution fusion | flops 5371330560 | bytes 12582912 | tf_op jit(solution)/shard_map/nch,dch->nd/dot_general | solution.py:74
  171.7 0.0 reduce-scatter.2.cloned.1.call-update
  171.7 0.0 all-reduce.5.cloned.1.call-done
  171.8 2.2 fusion.12
  173.9 0.8 copy.27
  174.8 3.7 %all-to-all-start.3 = ((bf16[16,2,16,512]{3,2,1,0:T(8,128)(2,1)}), bf16[16,2,16,512]{3,2,1,0:T(8,128)(2,1)S(1)}, u32[]{:S(2)}, u32[]{:S(2)}) async-start(bf16[16,2,16,512]{3,2,1,0:T(8,128)(2,1)} %bitcast.30), calls=%async_computation.4 | async-start | bytes 1048576 | tf_op jit(solution)/shard_map/all_to_all | solution.py:96
  178.5 0.0 all-reduce.3.cloned.1.call-done
  178.5 4.2 %fusion.2 = bf16[4,2,1280,64]{2,3,1,0:T(8,128)(2,1)} fusion(bf16[4,256,2,64]{1,3,2,0:T(8,128)(2,1)} %all-reduce.3.cloned.1.call-done, bf16[4,256,1280,1]{2,1,3,0:T(8,128)(2,1)} %bitcast.82), kind=kOutput, calls=%fused_computation.9 | convolution fusion | flops 336855040 | bytes 4194304 | tf_op jit(solution)/shard_map/mky,mkzl->mzyl/dot_general | solution.py:68
  182.7 3.7 %copy.23 = bf16[4,2,1280,64]{3,2,1,0:T(8,128)(2,1)} copy(bf16[4,2,1280,64]{2,3,1,0:T(8,128)(2,1)} %fusion.2) | data formatting | bytes 2621440 | tf_op jit(solution)/shard_map/convert_element_type | solution.py:94
  186.4 4.8 %convert_element_type.64 = bf16[4,2,4,20480]{3,2,1,0:T(4,128)(2,1)} reshape(bf16[4,2,1280,64]{3,2,1,0:T(8,128)(2,1)} %copy.23) | data formatting | bytes 2621440 | tf_op jit(solution)/shard_map/convert_element_type | solution.py:94
  191.2 0.0 copy-start.3
  191.2 3.8 %copy.24 = bf16[4,4,2,20480]{3,2,1,0:T(2,128)(2,1)} copy(bf16[4,4,2,20480]{3,0,2,1:T(4,128)(2,1)} %bitcast.86) | data formatting | bytes 2621440 | tf_op jit(solution)/shard_map/convert_element_type | solution.py:94
  194.9 0.0 all-to-all-done.3
  194.9 0.0 copy-start.2
  194.9 4.8 %all-to-all-start.2 = ((bf16[16,2,20480]{2,1,0:T(2,128)(2,1)}), bf16[16,2,20480]{2,1,0:T(2,128)(2,1)}, u32[]{:S(2)}, u32[]{:S(2)}) async-start(bf16[16,2,20480]{2,1,0:T(2,128)(2,1)} %bitcast.83), calls=%async_computation.3 | async-start | bytes 2621440 | tf_op jit(solution)/shard_map/all_to_all | solution.py:93
  199.7 0.0 copy-done.3
  199.8 3.3 %bitcast_multiply_fusion = f32[4,256,1280]{2,1,0:T(8,128)} fusion(bf16[4,256,2,64]{1,3,2,0:T(8,128)(2,1)S(1)} %copy-done.3, bf16[4,2,1280,64]{3,2,1,0:T(8,128)(2,1)S(1)} %reshape.128), kind=kOutput, calls=%fused_computation.6 | convolution fusion | flops 336855040 | bytes 6815744 | tf_op jit(solution)/shard_map/oyet,oemt->oym/dot_general | solution.py:64
  203.0 0.0 copy-done.2
  203.0 2.1 convolution_convert_fusion.1
  205.2 3.4 %copy.30 = bf16[96,2,16,512]{3,2,1,0:T(8,128)(2,1)} copy(bf16[96,2,16,512]{3,0,2,1:T(8,128)(2,1)S(1)} %convolution_convert_fusion.1) | data formatting | bytes 6291456
  208.6 22.6 %all-to-all-done.2 = bf16[16,2,20480]{2,1,0:T(2,128)(2,1)} async-done(((bf16[16,2,20480]{2,1,0:T(2,128)(2,1)}), bf16[16,2,20480]{2,1,0:T(2,128)(2,1)}, u32[]{:S(2)}, u32[]{:S(2)}) %all-to-all-start.2) | async-done | bytes 1310752 | tf_op jit(solution)/shard_map/all_to_all | solution.py:93
  231.2 3.6 %convolution_convert_fusion = bf16[96,2,20480]{2,0,1:T(8,128)(2,1)S(1)} fusion(s32[16]{0:T(128)S(1)} %copy-done.4, bf16[2,8,2,20480]{3,2,1,0:T(2,128)(2,1)} %bitcast.38), kind=kOutput, calls=%fused_computation.2 | convolution fusion | flops 129762816 | bytes 9175104 | tf_op jit(solution)/shard_map/dot_general | solution.py:103
  234.8 31.1 %copy.29 = bf16[96,2,20480]{2,1,0:T(2,128)(2,1)} copy(bf16[96,2,20480]{2,0,1:T(8,128)(2,1)S(1)} %convolution_convert_fusion) | data formatting | bytes 15728640
  265.9 0.0 reduce-scatter.2.cloned.1.call-done
  265.9 0.0 copy-start.1
  265.9 5.5 %fusion = bf16[1024,1280]{1,0:T(8,128)(2,1)} fusion(f32[4,256,1280]{2,1,0:T(8,128)} %bitcast_multiply_fusion, bf16[1024,1280]{1,0:T(8,128)(2,1)} %reduce-scatter.2.cloned.1.call-done), kind=kLoop, calls=%fused_computation.5 | loop fusion | flops 3932160 | bytes 10485760 | tf_op jit(solution)/shard_map/convert_element_type | solution.py:83
  271.4 0.0 copy-done.1
  (4 shorter events, 0.1 us)
Async XLA Ops:
  8.0 9.9 %copy-start = (bf16[96,2,16,512]{3,2,1,0:T(8,128)(2,1)S(1)}, bf16[96,2,16,512]{3,2,1,0:T(8,128)(2,1)}, u32[]{:S(2)}) copy-start(bf16[96,2,16,512]{3,2,1,0:T(8,128)(2,1)} %param.13) | copy-start | bytes 9437188
  8.0 98.8 %all-gather.3.cloned.1.call-start = ((), (), s32[]{:S(2)}) async-start(), calls=%async_computation.5 | async-start | bytes 3145728 | tf_op jit(solution)/shard_map/all_gather | solution.py:39
  15.2 2.7 copy-start.4
  15.2 146.2 %all-gather.5.cloned.1.call-start = ((), (), s32[]{:S(2)}) async-start(), calls=%async_computation.6 | async-start | bytes 6553600 | tf_op jit(solution)/shard_map/all_gather | solution.py:77
  21.3 20.8 %all-to-all-start = ((bf16[16,2,16,512]{3,2,1,0:T(8,128)(2,1)}), bf16[16,2,16,512]{3,2,1,0:T(8,128)(2,1)S(1)}, u32[]{:S(2)}, u32[]{:S(2)}) async-start(bf16[16,2,16,512]{3,2,1,0:T(8,128)(2,1)} %broadcast_select_fusion.1), calls=%async_computation.1 | async-start | bytes 1048576 | tf_op jit(solution)/shard_map/all_to_all | solution.py:44
  42.1 55.5 %all-to-all-start.1 = ((bf16[16,2,20480]{2,1,0:T(2,128)(2,1)}), bf16[16,2,20480]{2,1,0:T(2,128)(2,1)S(1)}, u32[]{:S(2)}, u32[]{:S(2)}) async-start(bf16[16,2,20480]{2,1,0:T(2,128)(2,1)} %broadcast_select_fusion), calls=%async_computation.2 | async-start | bytes 2621440 | tf_op jit(solution)/shard_map/all_to_all | solution.py:43
  45.6 126.1 %all-reduce.5.cloned.1.call-start = ((), (), s32[]{:S(2)}) async-start(), calls=%async_computation.9 | async-start | bytes 524288 | tf_op jit(solution)/shard_map/psum | solution.py:63
  106.7 71.8 %all-reduce.3.cloned.1.call-start = ((), (), s32[]{:S(2)}) async-start(), calls=%async_computation.8 | async-start | bytes 524288 | tf_op jit(solution)/shard_map/psum | solution.py:62
  109.9 156.1 %reduce-scatter.2.cloned.1.call-start = ((), (), s32[]{:S(2)}) async-start(), calls=%async_computation.7 | async-start | bytes 7864320 | tf_op jit(solution)/shard_map/reduce_scatter | solution.py:80
  174.8 20.2 %all-to-all-start.3 = ((bf16[16,2,16,512]{3,2,1,0:T(8,128)(2,1)}), bf16[16,2,16,512]{3,2,1,0:T(8,128)(2,1)S(1)}, u32[]{:S(2)}, u32[]{:S(2)}) async-start(bf16[16,2,16,512]{3,2,1,0:T(8,128)(2,1)} %bitcast.30), calls=%async_computation.4 | async-start | bytes 1048576 | tf_op jit(solution)/shard_map/all_to_all | solution.py:96
  191.2 8.6 %copy-start.3 = (bf16[4,256,2,64]{1,3,2,0:T(8,128)(2,1)S(1)}, bf16[4,256,2,64]{1,3,2,0:T(8,128)(2,1)}, u32[]{:S(2)}) copy-start(bf16[4,256,2,64]{1,3,2,0:T(8,128)(2,1)} %all-reduce.3.cloned.1.call-done) | copy-start | bytes 786436
  194.9 8.1 %copy-start.2 = (bf16[16,2,16,512]{3,2,1,0:T(8,128)(2,1)}, bf16[16,2,16,512]{3,2,1,0:T(8,128)(2,1)S(1)}, u32[]{:S(2)}) copy-start(bf16[16,2,16,512]{3,2,1,0:T(8,128)(2,1)S(1)} %all-to-all-done.3) | copy-start | bytes 1572868
  194.9 36.3 %all-to-all-start.2 = ((bf16[16,2,20480]{2,1,0:T(2,128)(2,1)}), bf16[16,2,20480]{2,1,0:T(2,128)(2,1)}, u32[]{:S(2)}, u32[]{:S(2)}) async-start(bf16[16,2,20480]{2,1,0:T(2,128)(2,1)} %bitcast.83), calls=%async_computation.3 | async-start | bytes 2621440 | tf_op jit(solution)/shard_map/all_to_all | solution.py:93
  265.9 5.5 %copy-start.1 = (bf16[96,2,16,512]{3,2,1,0:T(8,128)(2,1)S(1)}, bf16[96,2,16,512]{3,2,1,0:T(8,128)(2,1)}, u32[]{:S(2)}) copy-start(bf16[96,2,16,512]{3,2,1,0:T(8,128)(2,1)} %param.13) | copy-start | bytes 9437188
Sparse Core Ops, SparseCore 0:
  15.4 35.8 all-gather.2
  53.3 108.0 all-gather.4
Sparse Core Ops, SparseCore 1:
  106.8 36.6 all-reduce.4
  146.3 17.9 all-reduce.2
  171.8 12.2 reduce-scatter.1
where the time goes:
time: 280 us; the launch traced here: 279 us
  waiting for transfers between devices  132 us (47%)
  local copies, waits for them, and re-layouts  65.2 us (23%)
  matrix products  32.1 us (11%)
  starting transfers between devices  18.6 us (7%)
  between operations  15.8 us (6%)
  other arithmetic  15.4 us (6%)
    all_to_all x1, waiting for transfers between devices, on_device(): lax.all_to_all(departing_down, 'fsdp', split_axis=0, concat_axis=0, tiled...  51.9 us
    all_gather x1, waiting for transfers between devices, on_device(): lax.all_gather(key_value_weight, 'fsdp', axis=0, tiled=True)  51.5 us
    unnamed x13, local copies, waits for them, and re-layouts  37.1 us
    all_to_all x1, waiting for transfers between devices, on_device(): lax.all_to_all(send_down.astype(jnp.bfloat16), 'fsdp', split_axis=0, conc...  22.6 us
    convert_element_type x3, local copies, waits for them, and re-layouts, on_device(): send_down.astype(jnp.bfloat16)  12.3 us
    dot_general x1, matrix products, on_device(): jnp.einsum('nch,dch->nd', cot_full, lax.all_gather(key_value_weight, 'fsd...  10.3 us
    gather x1, local copies, waits for them, and re-layouts, on_device(): departing_down = jnp.take(adapter_first_factor, adapter_of_block, axis=0)  6.44 us
    all_to_all x1, starting transfers between devices, on_device(): lax.all_to_all(departing_up, 'fsdp', split_axis=0, concat_axis=0, tiled=T...  6.32 us
  transfers between devices with their start and end apart: 9, of which 4 were waited for; matrix products, arithmetic and copies ran while one was open for 36% of the time, Pallas kernels for 0%

commit v1 on v0

--- a/solution.py
+++ b/solution.py
@@ -1,6 +1,8 @@
 import jax
 import jax.numpy as jnp
 from jax import lax
+from jax.experimental import pallas as pl
+from jax.experimental.pallas import tpu as pltpu
 from jax.sharding import PartitionSpec as P
 
 ADAPTER_TOTAL = 96
@@ -11,7 +13,7 @@
 adapter_scale = 2.0
 
 
-def on_device(
+def general_on_device(
     acts,
     cotangent,
     key_value_weight,
@@ -111,6 +113,514 @@
     return (input_gradient, down_grad, up_grad)
 
 
+MESH = pl.DeviceIdType.MESH
+F32 = jnp.float32
+BF16 = jnp.bfloat16
+
+
+def product(left, right, left_dim, right_dim):
+    return lax.dot_general(
+        left, right, (((left_dim,), (right_dim,)), ((), ())), preferred_element_type=F32
+    )
+
+
+def trade_pairs(table):
+    rows = table.shape[0]
+    groups = table.reshape(rows // 8, 8, 128)
+    row_odd = lax.broadcasted_iota(jnp.int32, groups.shape, 1) % 2
+    lane_high = lax.broadcasted_iota(jnp.int32, groups.shape, 2) // 64
+    other = jnp.where(row_odd == 0, pltpu.roll(groups, 7, 1), pltpu.roll(groups, 1, 1))
+    other = pltpu.roll(other, 64, 2)
+    return jnp.where(row_odd == lane_high, groups, other).reshape(rows, 128)
+
+
+def pick_kernel(ids_ref, first_ref, second_ref, first_out, second_out, first_sem, second_sem):
+    copies = []
+    for block in range(first_out.shape[0]):
+        which = ids_ref[block]
+        copies.append(
+            pltpu.make_async_copy(second_ref.at[which], second_out.at[block], second_sem.at[block])
+        )
+        copies.append(
+            pltpu.make_async_copy(first_ref.at[which], first_out.at[block], first_sem.at[block])
+        )
+    for copy in copies:
+        copy.start()
+    for copy in copies:
+        copy.wait()
+
+
+def table_kernel(
+    ids_ref, down_ref, up_ref, down_out, up_out,
+    zero_down, zero_up, sum_down, sum_up, total_down, total_up, first, zero_sem, row_sem,
+):
+    blocks = down_ref.shape[0]
+    span = zero_down.shape[0]
+    steps = down_out.shape[0] // span
+    zero_down[...] = jnp.zeros_like(zero_down)
+    zero_up[...] = jnp.zeros_like(zero_up)
+    copies = []
+    for step in range(steps):
+        rows = pl.ds(step * span, span)
+        copies.append(pltpu.make_async_copy(zero_down, down_out.at[rows], zero_sem.at[0, step]))
+        copies.append(pltpu.make_async_copy(zero_up, up_out.at[rows], zero_sem.at[1, step]))
+    for copy in copies:
+        copy.start()
+
+    def add_up(block, carry):
+        mine = ids_ref[block]
+        before = lax.fori_loop(
+            0, block, lambda i, n: n + (ids_ref[i] == mine).astype(jnp.int32), jnp.int32(0)
+        )
+        first[block] = before
+
+        @pl.when(before == 0)
+        def _():
+            total_down[...] = down_ref[block].astype(F32)
+            total_up[...] = up_ref[:, block].astype(F32)
+
+            def later(i, c):
+                @pl.when(ids_ref[i] == mine)
+                def _():
+                    total_down[...] += down_ref[i].astype(F32)
+                    total_up[...] += up_ref[:, i].astype(F32)
+                return c
+
+            lax.fori_loop(block + 1, blocks, later, 0)
+            sum_down[block] = total_down[...].astype(BF16)
+            sum_up[block] = total_up[...].astype(BF16)
+        return carry
+
+    lax.fori_loop(0, blocks, add_up, 0)
+    for copy in copies:
+        copy.wait()
+
+    def rows_of(block):
+        which = ids_ref[block]
+        return (
+            pltpu.make_async_copy(sum_down.at[block], down_out.at[which], row_sem.at[0, block]),
+            pltpu.make_async_copy(sum_up.at[block], up_out.at[which], row_sem.at[1, block]),
+        )
+
+    def send(block, carry):
+        @pl.when(first[block] == 0)
+        def _():
+            for copy in rows_of(block):
+                copy.start()
+        return carry
+
+    def settle(block, carry):
+        @pl.when(first[block] == 0)
+        def _():
+            for copy in rows_of(block):
+                copy.wait()
+        return carry
+
+    lax.fori_loop(0, blocks, send, 0)
+    lax.fori_loop(0, blocks, settle, 0)
+
+
+def layer_kernel(
+    cot_ref, w_ref, first_ref, second_ref, acts_ref,
+    ig_ref, down_ref, up_ref,
+    cot, weight, first, first_rows, second, acts,
+    head_part, head_got, head, low_part, low_got, low_sum, low,
+    down_stage, up_stage, part, part_got,
+    local_sem, b_send, b_recv, a_send, a_recv, d_send, d_recv, u_send, u_recv,
+    c_send, c_recv, h_send, h_recv, l_send, l_recv,
+    w_send, w_recv, y_send, y_recv, p_send, p_recv, x_send, x_recv,
+):
+    f = lax.axis_index("fsdp")
+    g = lax.axis_index("groups")
+    t = lax.axis_index("tensor")
+    a = lax.axis_index("adapter")
+    other_g, other_t, other_a = 1 - g, 1 - t, 1 - a
+    near = f + 1 - 2 * (f % 2)
+    peers = (near, 2 - f // 2, 3 - 3 * (f // 2))
+    inner = f * (3 - f) > 0
+    blocks = 4
+    portion = first_ref.shape[1]
+    ranks = second_ref.shape[2]
+    quarter = cot_ref.shape[1]
+    half_rows = w_ref.shape[1] // 2
+    pending = []
+
+    def remote(source, target, send_sem, recv_sem, **where):
+        return pltpu.make_async_remote_copy(
+            src_ref=source, dst_ref=target, send_sem=send_sem, recv_sem=recv_sem,
+            device_id=where, device_id_type=MESH,
+        )
+
+    def go(copy):
+        copy.start()
+        pending.append(copy)
+
+    barrier = pltpu.get_barrier_semaphore()
+    for where in (
+        {"fsdp": peers[0]}, {"fsdp": peers[1]}, {"fsdp": peers[2]},
+        {"groups": other_g}, {"tensor": other_t}, {"adapter": other_a},
+    ):
+        pl.semaphore_signal(barrier, inc=1, device_id=where, device_id_type=MESH)
+
+    my_blocks = pl.ds(f * blocks, blocks)
+    my_ranks = pl.ds(pl.multiple_of(f * ranks, 16), ranks)
+    my_quarter = pl.ds(pl.multiple_of(a * quarter, 256), quarter)
+    other_quarter = pl.ds(pl.multiple_of(other_a * quarter, 256), quarter)
+    own = [
+        pltpu.make_async_copy(second_ref.at[my_blocks, a], second.at[:, my_ranks], local_sem.at[0]),
+        pltpu.make_async_copy(cot_ref, cot.at[:, my_quarter], local_sem.at[1]),
+        pltpu.make_async_copy(acts_ref, acts, local_sem.at[2]),
+        pltpu.make_async_copy(w_ref, weight.at[f], local_sem.at[3]),
+        pltpu.make_async_copy(first_ref.at[my_blocks], first.at[f], local_sem.at[4]),
+    ]
+    for copy in own:
+        copy.start()
+    pl.semaphore_wait(barrier, 6)
+
+    for i, peer in enumerate(peers):
+        go(remote(
+            second_ref.at[pl.ds(peer * blocks, blocks), a], second.at[:, my_ranks],
+            b_send.at[i], b_recv.at[f], fsdp=peer,
+        ))
+    for c in (other_a, a):
+        go(remote(
+            cot_ref.at[c], cot.at[c, my_quarter], c_send.at[c], c_recv.at[c], adapter=other_a
+        ))
+    for i, peer in enumerate(peers):
+        go(remote(
+            first_ref.at[pl.ds(peer * blocks, blocks)], first.at[f],
+            a_send.at[i], a_recv.at[f], fsdp=peer,
+        ))
+
+    def piece(s, c, sub):
+        return weight.at[s, c, pl.ds(sub * half_rows, half_rows)]
+
+    def weight_copy(s, sub, slot, target):
+        return remote(
+            piece(s, g, sub), piece(s, g, sub), w_send.at[slot, sub], w_recv.at[s, sub], fsdp=target
+        )
+
+    def twin_copy(s, c, j, sub):
+        return remote(
+            piece(s, c, sub), piece(s, c, sub), y_send.at[j, sub], y_recv.at[s, sub], groups=other_g
+        )
+
+    onward = (3 - f, (f - 1) * 3, (f - 1) * 3)
+
+    def pass_on(j):
+        s = peers[j]
+        for sub in range(2):
+            weight_copy(s, sub, 0, near).wait_recv()
+
+            @pl.when(inner)
+            def _():
+                weight_copy(s, sub, 2 + j, onward[j]).start()
+
+            go(twin_copy(s, g, j, sub))
+
+    own[3].wait()
+    for sub in range(2):
+        go(weight_copy(f, sub, 0, near))
+
+        @pl.when(inner)
+        def _():
+            weight_copy(f, sub, 1, 3 - f).start()
+
+    own[0].wait()
+    own[1].wait()
+    for i, peer in enumerate(peers):
+        remote(
+            second_ref.at[pl.ds(peer * blocks, blocks), a],
+            second.at[:, pl.ds(pl.multiple_of(peer * ranks, 16), ranks)],
+            b_send.at[i], b_recv.at[peer], fsdp=peer,
+        ).wait_recv()
+
+    def cot_arrival(c):
+        remote(
+            cot_ref.at[c], cot.at[c, other_quarter], c_send.at[c], c_recv.at[c], adapter=other_a
+        ).wait_recv()
+
+    def columns(b):
+        return pl.ds(pl.multiple_of(b * BLOCK, BLOCK), BLOCK)
+
+    cot_arrival(a)
+
+    def head_block(b, carry):
+        head_part[:, columns(b)] = product(second[b], cot[a, columns(b)], 1, 1).astype(BF16)
+        return carry
+
+    lax.fori_loop(0, blocks, head_block, 0)
+    swap = remote(head_part, head_got, h_send.at[0], h_recv.at[0], tensor=other_t)
+    go(swap)
+    swap.wait_recv()
+    head[a] = (head_part[...].astype(F32) + head_got[...].astype(F32)).astype(BF16)
+    go(remote(head.at[a], head.at[a], h_send.at[1], h_recv.at[1], adapter=other_a))
+    own[2].wait()
+    remote(head.at[other_a], head.at[other_a], h_send.at[1], h_recv.at[1], adapter=other_a).wait_recv()
+
+    def head_of(b):
+        return head[:, :, columns(b)].reshape(2 * ADAPTER_RANK, BLOCK)
+
+    def down_block(b, carry):
+        entries = product(head_of(b), acts[columns(b)], 1, 0)
+        down_stage[b] = trade_pairs((adapter_scale * entries).T).astype(BF16)
+        return carry
+
+    lax.fori_loop(0, blocks, down_block, 0)
+
+    def entries_for(device):
+        return down_stage.at[:, pl.ds(pl.multiple_of(device * portion, 16), portion)]
+
+    for i, peer in enumerate(peers):
+        go(remote(
+            entries_for(peer), down_ref.at[my_blocks], d_send.at[i], d_recv.at[f], fsdp=peer
+        ))
+    keep_down = pltpu.make_async_copy(entries_for(f), down_ref.at[my_blocks], local_sem.at[5])
+    keep_down.start()
+
+    cot_arrival(other_a)
+
+    def part_copy(s, h):
+        return remote(part.at[s], part_got.at[h], p_send.at[h], p_recv.at[h], tensor=other_t)
+
+    def frozen(s):
+        def rows(b, carry):
+            value = product(cot[0, columns(b)], weight[s, 0], 1, 1)
+            value = value + product(cot[1, columns(b)], weight[s, 1], 1, 1)
+            part[s, columns(b)] = value.astype(BF16)
+            return carry
+
+        lax.fori_loop(0, blocks, rows, 0)
+
+        @pl.when(s // 2 != t)
+        def _():
+            part_copy(s, s % 2).start()
+
+    frozen(f)
+
+    own[4].wait()
+    for i, peer in enumerate(peers):
+        remote(
+            first_ref.at[my_blocks], first.at[peer], a_send.at[i], a_recv.at[peer], fsdp=peer
+        ).wait_recv()
+
+    def first_block(n, carry):
+        b, s = n // 4, n % 4
+        first_rows[b, pl.ds(pl.multiple_of(s * portion, 16), portion)] = trade_pairs(
+            first[s, b].astype(F32)
+        ).astype(BF16)
+        return carry
+
+    lax.fori_loop(0, 4 * blocks, first_block, 0)
+
+    def low_block(b, carry):
+        value = product(acts[columns(b)], first_rows[b], 1, 0)
+        low_part[:, :, columns(b)] = value.T.reshape(2, ADAPTER_RANK, BLOCK).astype(BF16)
+        return carry
+
+    lax.fori_loop(0, blocks, low_block, 0)
+    swap = remote(low_part.at[other_a], low_got.at[0], l_send.at[0], l_recv.at[0], adapter=other_a)
+    go(swap)
+    pass_on(0)
+    swap.wait_recv()
+    low_sum[...] = (low_part[a].astype(F32) + low_got[0].astype(F32)).astype(BF16)
+    swap = remote(low_sum, low_got.at[1], l_send.at[1], l_recv.at[1], tensor=other_t)
+    go(swap)
+    swap.wait_recv()
+    low[...] = (low_sum[...].astype(F32) + low_got[1].astype(F32)).astype(BF16)
+
+    def up_block(b, carry):
+        value = adapter_scale * product(low[:, columns(b)], cot[a, columns(b)], 1, 0)
+        up_stage[b] = value.astype(BF16)
+        return carry
+
+    lax.fori_loop(0, blocks, up_block, 0)
+
+    def ranks_for(device):
+        return up_stage.at[:, pl.ds(pl.multiple_of(device * ranks, 16), ranks)]
+
+    for i, peer in enumerate(peers):
+        go(remote(ranks_for(peer), up_ref.at[a, my_blocks], u_send.at[i], u_recv.at[f], fsdp=peer))
+    keep_up = pltpu.make_async_copy(ranks_for(f), up_ref.at[a, my_blocks], local_sem.at[6])
+    keep_up.start()
+
+    def twin_arrival(j):
+        for sub in range(2):
+            twin_copy(peers[j], other_g, j, sub).wait_recv()
+
+    pass_on(1)
+    twin_arrival(0)
+    frozen(peers[0])
+    pass_on(2)
+    keep_up.wait()
+    for i, peer in enumerate(peers):
+        there = up_ref.at[a, pl.ds(peer * blocks, blocks)]
+        remote(ranks_for(peer), there, u_send.at[i], u_recv.at[peer], fsdp=peer).wait_recv()
+    go(remote(up_ref.at[a], up_ref.at[a], x_send.at[0], x_recv.at[0], adapter=other_a))
+    twin_arrival(1)
+    frozen(peers[1])
+    twin_arrival(2)
+    frozen(peers[2])
+
+    for h in range(2):
+        part_copy(2 * t + h, h).wait_recv()
+    width = part.shape[2]
+
+    def final_block(b, carry):
+        grad = head_of(b).astype(F32).T.astype(BF16)
+        for h in range(2):
+            term = product(grad, first_rows[b, pl.ds(h * width, width)], 1, 1)
+            base = part[2 * t + h, columns(b)].astype(F32) + part_got[h, columns(b)].astype(F32)
+            ig_ref[columns(b), pl.ds(h * width, width)] = (base + adapter_scale * term).astype(BF16)
+        return carry
+
+    lax.fori_loop(0, blocks, final_block, 0)
+
+    keep_down.wait()
+    for i, peer in enumerate(peers):
+        remote(
+            entries_for(peer), down_ref.at[pl.ds(peer * blocks, blocks)],
+            d_send.at[i], d_recv.at[peer], fsdp=peer,
+        ).wait_recv()
+    remote(up_ref.at[other_a], up_ref.at[other_a], x_send.at[0], x_recv.at[0], adapter=other_a).wait_recv()
+    for h in range(2):
+        part_copy(2 * other_t + h, h).wait_send()
+    for copy in pending:
+        copy.wait_send()
+
+    @pl.when(inner)
+    def _():
+        for sub in range(2):
+            weight_copy(f, sub, 1, 3 - f).wait_send()
+            for j in range(3):
+                weight_copy(peers[j], sub, 2 + j, onward[j]).wait_send()
+
+
+def slice_on_device(
+    acts,
+    cotangent,
+    key_value_weight,
+    adapter_first_factor,
+    adapter_second_factor,
+    adapter_of_block,
+    occupied_rows,
+):
+    f = lax.axis_index("fsdp")
+    a = lax.axis_index("adapter")
+    quarter, _, head_half = cotangent.shape
+    rows, features = acts.shape
+    blocks = rows // BLOCK
+    all_blocks = adapter_of_block.shape[0]
+    total, _, length = adapter_first_factor.shape
+    ranks = adapter_second_factor.shape[2]
+    portion = length // ADAPTER_RANK
+    shard = key_value_weight.shape[0]
+    anywhere = pl.BlockSpec(memory_space=pl.ANY)
+    in_vmem = pl.BlockSpec(memory_space=pltpu.VMEM)
+    in_smem = pl.BlockSpec(memory_space=pltpu.SMEM)
+    dma = pltpu.SemaphoreType.DMA
+
+    quarter_blocks = quarter // BLOCK
+    live = lax.dynamic_slice_in_dim(
+        occupied_rows, f * blocks + a * quarter_blocks, quarter_blocks, 0
+    )
+    kept = jnp.arange(BLOCK, dtype=jnp.int32)[None, :] < live[:, None]
+    masked = jnp.where(
+        kept[:, :, None, None],
+        cotangent.reshape(quarter_blocks, BLOCK, 2, head_half),
+        jnp.zeros((), BF16),
+    )
+    masked = masked.reshape(quarter, 2, head_half).transpose(1, 0, 2)
+    weight = key_value_weight.transpose(1, 0, 2)
+
+    first_used, second_used = pl.pallas_call(
+        pick_kernel,
+        out_shape=(
+            jax.ShapeDtypeStruct((all_blocks, 2, length), BF16),
+            jax.ShapeDtypeStruct((all_blocks, 2, ranks, head_half), BF16),
+        ),
+        in_specs=[in_smem, anywhere, anywhere],
+        out_specs=(anywhere, anywhere),
+        scratch_shapes=[dma((all_blocks,)), dma((all_blocks,))],
+        name="pick",
+    )(adapter_of_block, adapter_first_factor, adapter_second_factor)
+    first_used = first_used.reshape(all_blocks, 2, length // 128, 128).transpose(0, 2, 1, 3)
+    first_used = first_used.reshape(all_blocks, portion, 128)
+
+    input_gradient, back_down, back_up = pl.pallas_call(
+        layer_kernel,
+        out_shape=(
+            jax.ShapeDtypeStruct((rows, features), BF16),
+            jax.ShapeDtypeStruct((all_blocks, portion, 128), BF16),
+            jax.ShapeDtypeStruct((2, all_blocks, ranks, head_half), BF16),
+        ),
+        in_specs=[anywhere] * 5,
+        out_specs=(in_vmem, anywhere, anywhere),
+        scratch_shapes=[
+            pltpu.VMEM((2, rows, head_half), BF16),
+            pltpu.VMEM((4, 2, shard, head_half), BF16),
+            pltpu.VMEM((4, blocks, portion, 128), BF16),
+            pltpu.VMEM((blocks, features, 128), BF16),
+            pltpu.VMEM((blocks, ADAPTER_RANK, head_half), BF16),
+            pltpu.VMEM((rows, features), BF16),
+            pltpu.VMEM((ADAPTER_RANK, rows), BF16),
+            pltpu.VMEM((ADAPTER_RANK, rows), BF16),
+            pltpu.VMEM((2, ADAPTER_RANK, rows), BF16),
+            pltpu.VMEM((2, ADAPTER_RANK, rows), BF16),
+            pltpu.VMEM((2, ADAPTER_RANK, rows), BF16),
+            pltpu.VMEM((ADAPTER_RANK, rows), BF16),
+            pltpu.VMEM((ADAPTER_RANK, rows), BF16),
+            pltpu.VMEM((blocks, features, 128), BF16),
+            pltpu.VMEM((blocks, ADAPTER_RANK, head_half), BF16),
+            pltpu.VMEM((4, rows, shard), BF16),
+            pltpu.VMEM((2, rows, shard), BF16),
+            dma((7,)),
+            dma((3,)), dma((4,)), dma((3,)), dma((4,)),
+            dma((3,)), dma((4,)), dma((3,)), dma((4,)),
+            dma((2,)), dma((2,)), dma((2,)), dma((2,)), dma((2,)), dma((2,)),
+            dma((5, 2)), dma((4, 2)), dma((3, 2)), dma((4, 2)),
+            dma((2,)), dma((2,)), dma((1,)), dma((1,)),
+        ],
+        compiler_params=pltpu.CompilerParams(
+            collective_id=0, has_side_effects=True, vmem_limit_bytes=50 * 2**20
+        ),
+        name="layer",
+    )(masked, weight, first_used, second_used, acts)
+
+    span = 8
+    down_grad, up_grad = pl.pallas_call(
+        table_kernel,
+        out_shape=(
+            jax.ShapeDtypeStruct((total, portion, 128), BF16),
+            jax.ShapeDtypeStruct((total, 2, ranks, head_half), BF16),
+        ),
+        in_specs=[in_smem, in_vmem, in_vmem],
+        out_specs=(anywhere, anywhere),
+        scratch_shapes=[
+            pltpu.VMEM((span, portion, 128), BF16),
+            pltpu.VMEM((span, 2, ranks, head_half), BF16),
+            pltpu.VMEM((all_blocks, portion, 128), BF16),
+            pltpu.VMEM((all_blocks, 2, ranks, head_half), BF16),
+            pltpu.VMEM((portion, 128), F32),
+            pltpu.VMEM((2, ranks, head_half), F32),
+            pltpu.SMEM((all_blocks,), jnp.int32),
+            dma((2, total // span)),
+            dma((2, all_blocks)),
+        ],
+        compiler_params=pltpu.CompilerParams(vmem_limit_bytes=32 * 2**20),
+        name="table",
+    )(adapter_of_block, back_down, back_up)
+    down_grad = down_grad.reshape(total, length // 128, 2, 128).transpose(0, 2, 1, 3)
+    return (input_gradient, down_grad.reshape(total, 2, length), up_grad)
+
+
+def on_slice(*args):
+    sizes = tuple(lax.axis_size(name) for name in ("groups", "fsdp", "tensor", "adapter"))
+    if sizes == (2, 4, 2, 2) and args[0].shape == (4 * BLOCK, 1280):
+        return slice_on_device(*args)
+    return general_on_device(*args)
+
+
 def solution(mesh):
     in_specs = (
         P(("groups", "fsdp"), ("adapter", "tensor")),
@@ -127,5 +637,5 @@
         P("groups", None, "fsdp", "tensor"),
     )
     return jax.shard_map(
-        on_device, mesh=mesh, in_specs=in_specs, out_specs=out_specs, check_vma=False
-    )
+        on_slice, mesh=mesh, in_specs=in_specs, out_specs=out_specs, check_vma=False
+    )

time: 280 us -> 197 us (0.70)
  Pallas kernels: 0 us -> 187 us
  waiting for transfers between devices: 132 us -> 0 us
  local copies, waits for them, and re-layouts: 65.2 us -> 6.56 us
  matrix products: 32.1 us -> 0 us
  starting transfers between devices: 18.6 us -> 0 us
  between operations: 15.8 us -> 0.7 us
  other arithmetic: 15.4 us -> 1.48 us
    pallas_call x0 -> x3, Pallas kernels: none -> 187 us  [the longest x1 123 us: slice_on_device(): pl.pallas_call(layer_kernel, out_shape=(jax.ShapeDtypeStruct((rows, featu...]
    all_to_all x4 -> x0, waiting for transfers between devices: 80.3 us -> none  [the longest x1 51.9 us: on_device(): lax.all_to_all(departing_down, 'fsdp', split_axis=0, concat_axis=0, tiled...]
    all_gather x2 -> x0, waiting for transfers between devices: 51.5 us -> none  [the longest x1 51.5 us: on_device(): lax.all_gather(key_value_weight, 'fsdp', axis=0, tiled=True)]
    dot_general x8 -> x0, matrix products: 32.1 us -> none  [the longest x1 10.3 us: on_device(): jnp.einsum('nch,dch->nd', cot_full, lax.all_gather(key_value_weight, 'fsd...]
    unnamed x13 -> x8, local copies, waits for them, and re-layouts: 37.1 us -> 5.71 us
    all_to_all x4 -> x0, starting transfers between devices: 18.4 us -> none  [the longest x1 6.32 us: on_device(): lax.all_to_all(departing_up, 'fsdp', split_axis=0, concat_axis=0, tiled=T...]
    convert_element_type x4 -> x0, local copies, waits for them, and re-layouts: 13.1 us -> none  [the longest x3 12.3 us: on_device(): send_down.astype(jnp.bfloat16)]
    gather x3 -> x0, local copies, waits for them, and re-layouts: 8.4 us -> none  [the longest x1 6.44 us: on_device(): departing_down = jnp.take(adapter_first_factor, adapter_of_block, axis=0)]
  transfers between devices with their start and end apart: 9 -> 0, of which waited for: 4 -> 0; matrix products, arithmetic and copies ran while one was open for 36% -> 0% of each run, Pallas kernels for 0% -> 0%
where the time goes in v1:
time: 197 us; the launch traced here: 196 us
  Pallas kernels  187 us (95%)
  local copies, waits for them, and re-layouts  6.56 us (3%)
    pallas_call x1, Pallas kernels, slice_on_device(): pl.pallas_call(layer_kernel, out_shape=(jax.ShapeDtypeStruct((rows, featu...  123 us
    pallas_call x1, Pallas kernels, slice_on_device(): pl.pallas_call(pick_kernel, out_shape=(jax.ShapeDtypeStruct((all_blocks,...  57.6 us
    pallas_call x1, Pallas kernels, slice_on_device(): pl.pallas_call(table_kernel, out_shape=(jax.ShapeDtypeStruct((total, port...  6.26 us
    unnamed x8, local copies, waits for them, and re-layouts  5.71 us

profile of v1, /device:TPU:0, one launch (start us, length us, event | category | flops | bytes accessed | tf_op | source)
XLA Modules:
  0.0 195.5 jit_solution(4471799984540737267)
XLA Ops:
  0.6 0.0 copy-start.2
  0.6 0.8 dynamic_slice.3
  1.5 0.1 iota_compare_fusion
  1.6 1.4 fusion.cot_ref
  3.0 0.0 copy-done.2
  3.0 1.3 copy.18
  4.3 57.6 %pick.1 = (bf16[16,2,20480]{2,1,0:T(2,128)(2,1)}, bf16[16,2,16,512]{3,2,1,0:T(8,128)(2,1)}) custom-call(s32[16]{0:T(128)} %ids_ref.3, bf16[96,2,20480]{2,1,0:T(2,128)(2,1)} %first_ref.1, bf16[96,2,16,512]{3,2,1,0:T(8,128)(2,1)} %second_ref.1), custom_call_target="tpu_custom_call" | custom-call | tf_op jit(solution)/shard_map/pick/pallas_call | solution.py:536
  61.9 0.0 copy-start
  61.9 1.0 copy-done
  63.0 0.0 copy-start.1
  63.0 122.9 %layer.1 = (bf16[1024,1280]{1,0:T(8,128)(2,1)}, bf16[16,320,128]{2,1,0:T(8,128)(2,1)S(1)}, bf16[2,16,16,512]{3,2,1,0:T(8,128)(2,1)S(1)}) custom-call(bf16[2,512,512]{2,1,0:T(8,128)(2,1)S(1)} %fusion.cot_ref, bf16[2,640,512]{2,1,0:T(8,128)(2,1)} %bitcast.15, bf16[16,320,128]{2,1,0:T(8,128)(2,1)} %bitcast.16, bf16[16,2,16,512]{3,2,1,0:T(8,128)(2,1)S(1)} %copy-done, ...), custom_call_target="tpu_custom_call" | custom-call | tf_op jit(solution)/shard_map/layer/pallas_call | solution.py:550
  185.8 0.0 copy-done.1
  185.9 6.3 %table.1 = (bf16[96,320,128]{2,1,0:T(8,128)(2,1)}, bf16[96,2,16,512]{3,2,1,0:T(8,128)(2,1)}) custom-call(s32[16]{0:T(128)S(1)} %copy-done.1, bf16[16,320,128]{2,1,0:T(8,128)(2,1)S(1)} %get-tuple-element.13.down_ref, bf16[2,16,16,512]{3,2,1,0:T(8,128)(2,1)S(1)} %get-tuple-element.14.up_ref), custom_call_target="tpu_custom_call" | custom-call | tf_op jit(solution)/shard_map/table/pallas_call | solution.py:591
  192.1 3.4 %copy.20 = bf16[1024,1280]{1,0:T(8,128)(2,1)} copy(bf16[1024,1280]{1,0:T(8,128)(2,1)} %get-tuple-element.20) | data formatting | bytes 5242880
  (1 shorter events, 0.0 us)
Async XLA Ops:
  0.6 2.4 %copy-start.2 = (bf16[640,2,512]{2,1,0:T(2,128)(2,1)S(1)}, bf16[640,2,512]{2,1,0:T(2,128)(2,1)}, u32[]{:S(2)}) copy-start(bf16[640,2,512]{2,1,0:T(2,128)(2,1)} %param.9) | copy-start | bytes 3932164
  61.9 1.0 copy-start
  63.0 122.9 %copy-start.1 = (s32[16]{0:T(128)S(1)}, s32[16]{0:T(128)}, u32[]{:S(2)}) copy-start(s32[16]{0:T(128)} %ids_ref.3) | copy-start | bytes 196

commit v2 on v1

--- a/solution.py
+++ b/solution.py
@@ -151,21 +151,32 @@
 
 
 def table_kernel(
-    ids_ref, down_ref, up_ref, down_out, up_out,
-    zero_down, zero_up, sum_down, sum_up, total_down, total_up, first, zero_sem, row_sem,
+    ids_ref, down_in, up_in, ig_ref, ig_out, down_out, up_out,
+    zero_down, zero_up, down_ref, up_ref,
+    ig, sum_down, sum_up, total_down, total_up, first, in_sem, ig_sem, zero_sem, row_sem,
 ):
     blocks = down_ref.shape[0]
     span = zero_down.shape[0]
-    steps = down_out.shape[0] // span
+    arrive = [
+        pltpu.make_async_copy(down_in, down_ref, in_sem.at[0]),
+        pltpu.make_async_copy(up_in, up_ref, in_sem.at[1]),
+    ]
+    take = pltpu.make_async_copy(ig_ref, ig, ig_sem.at[0])
+    give = pltpu.make_async_copy(ig, ig_out, ig_sem.at[1])
+    for copy in arrive:
+        copy.start()
+    take.start()
     zero_down[...] = jnp.zeros_like(zero_down)
     zero_up[...] = jnp.zeros_like(zero_up)
     copies = []
-    for step in range(steps):
+    for step in range(down_out.shape[0] // span):
         rows = pl.ds(step * span, span)
         copies.append(pltpu.make_async_copy(zero_down, down_out.at[rows], zero_sem.at[0, step]))
         copies.append(pltpu.make_async_copy(zero_up, up_out.at[rows], zero_sem.at[1, step]))
     for copy in copies:
         copy.start()
+    for copy in arrive:
+        copy.wait()
 
     def add_up(block, carry):
         mine = ids_ref[block]
@@ -191,6 +202,8 @@
             sum_up[block] = total_up[...].astype(BF16)
         return carry
 
+    take.wait()
+    give.start()
     lax.fori_loop(0, blocks, add_up, 0)
     for copy in copies:
         copy.wait()
@@ -218,6 +231,7 @@
 
     lax.fori_loop(0, blocks, send, 0)
     lax.fori_loop(0, blocks, settle, 0)
+    give.wait()
 
 
 def layer_kernel(
@@ -286,12 +300,6 @@
         go(remote(
             cot_ref.at[c], cot.at[c, my_quarter], c_send.at[c], c_recv.at[c], adapter=other_a
         ))
-    for i, peer in enumerate(peers):
-        go(remote(
-            first_ref.at[pl.ds(peer * blocks, blocks)], first.at[f],
-            a_send.at[i], a_recv.at[f], fsdp=peer,
-        ))
-
     def piece(s, c, sub):
         return weight.at[s, c, pl.ds(sub * half_rows, half_rows)]
 
@@ -361,6 +369,13 @@
     def head_of(b):
         return head[:, :, columns(b)].reshape(2 * ADAPTER_RANK, BLOCK)
 
+    pass_on(0)
+    for i, peer in enumerate(peers):
+        go(remote(
+            first_ref.at[pl.ds(peer * blocks, blocks)], first.at[f],
+            a_send.at[i], a_recv.at[f], fsdp=peer,
+        ))
+
     def down_block(b, carry):
         entries = product(head_of(b), acts[columns(b)], 1, 0)
         down_stage[b] = trade_pairs((adapter_scale * entries).T).astype(BF16)
@@ -370,13 +385,6 @@
 
     def entries_for(device):
         return down_stage.at[:, pl.ds(pl.multiple_of(device * portion, 16), portion)]
-
-    for i, peer in enumerate(peers):
-        go(remote(
-            entries_for(peer), down_ref.at[my_blocks], d_send.at[i], d_recv.at[f], fsdp=peer
-        ))
-    keep_down = pltpu.make_async_copy(entries_for(f), down_ref.at[my_blocks], local_sem.at[5])
-    keep_down.start()
 
     cot_arrival(other_a)
 
@@ -396,7 +404,22 @@
         def _():
             part_copy(s, s % 2).start()
 
+    def twin_arrival(j):
+        for sub in range(2):
+            twin_copy(peers[j], other_g, j, sub).wait_recv()
+
     frozen(f)
+    pass_on(1)
+    twin_arrival(0)
+    frozen(peers[0])
+    pass_on(2)
+    for i, peer in enumerate(peers):
+        go(remote(
+            entries_for(peer), down_ref.at[my_blocks], d_send.at[i], d_recv.at[f], fsdp=peer
+        ))
+    keep_down = pltpu.make_async_copy(entries_for(f), down_ref.at[my_blocks], local_sem.at[5])
+    keep_down.start()
+
 
     own[4].wait()
     for i, peer in enumerate(peers):
@@ -421,7 +444,6 @@
     lax.fori_loop(0, blocks, low_block, 0)
     swap = remote(low_part.at[other_a], low_got.at[0], l_send.at[0], l_recv.at[0], adapter=other_a)
     go(swap)
-    pass_on(0)
     swap.wait_recv()
     low_sum[...] = (low_part[a].astype(F32) + low_got[0].astype(F32)).astype(BF16)
     swap = remote(low_sum, low_got.at[1], l_send.at[1], l_recv.at[1], tensor=other_t)
@@ -444,23 +466,15 @@
     keep_up = pltpu.make_async_copy(ranks_for(f), up_ref.at[a, my_blocks], local_sem.at[6])
     keep_up.start()
 
-    def twin_arrival(j):
-        for sub in range(2):
-            twin_copy(peers[j], other_g, j, sub).wait_recv()
-
-    pass_on(1)
-    twin_arrival(0)
-    frozen(peers[0])
-    pass_on(2)
-    keep_up.wait()
-    for i, peer in enumerate(peers):
-        there = up_ref.at[a, pl.ds(peer * blocks, blocks)]
-        remote(ranks_for(peer), there, u_send.at[i], u_recv.at[peer], fsdp=peer).wait_recv()
-    go(remote(up_ref.at[a], up_ref.at[a], x_send.at[0], x_recv.at[0], adapter=other_a))
     twin_arrival(1)
     frozen(peers[1])
     twin_arrival(2)
     frozen(peers[2])
+    keep_up.wait()
+    for i, peer in enumerate(peers):
+        there = up_ref.at[a, pl.ds(peer * blocks, blocks)]
+        remote(ranks_for(peer), there, u_send.at[i], u_recv.at[peer], fsdp=peer).wait_recv()
+    go(remote(up_ref.at[a], up_ref.at[a], x_send.at[0], x_recv.at[0], adapter=other_a))
 
     for h in range(2):
         part_copy(2 * t + h, h).wait_recv()
@@ -540,13 +554,14 @@
             jax.ShapeDtypeStruct((all_blocks, 2, ranks, head_half), BF16),
         ),
         in_specs=[in_smem, anywhere, anywhere],
-        out_specs=(anywhere, anywhere),
+        out_specs=(in_vmem, in_vmem),
         scratch_shapes=[dma((all_blocks,)), dma((all_blocks,))],
         name="pick",
     )(adapter_of_block, adapter_first_factor, adapter_second_factor)
     first_used = first_used.reshape(all_blocks, 2, length // 128, 128).transpose(0, 2, 1, 3)
     first_used = first_used.reshape(all_blocks, portion, 128)
 
+    span = 8
     input_gradient, back_down, back_up = pl.pallas_call(
         layer_kernel,
         out_shape=(
@@ -582,34 +597,39 @@
             dma((2,)), dma((2,)), dma((1,)), dma((1,)),
         ],
         compiler_params=pltpu.CompilerParams(
-            collective_id=0, has_side_effects=True, vmem_limit_bytes=50 * 2**20
+            collective_id=0, has_side_effects=True, vmem_limit_bytes=58 * 2**20
         ),
         name="layer",
     )(masked, weight, first_used, second_used, acts)
 
-    span = 8
-    down_grad, up_grad = pl.pallas_call(
+    input_gradient, down_grad, up_grad = pl.pallas_call(
         table_kernel,
         out_shape=(
+            jax.ShapeDtypeStruct((rows, features), BF16),
             jax.ShapeDtypeStruct((total, portion, 128), BF16),
             jax.ShapeDtypeStruct((total, 2, ranks, head_half), BF16),
         ),
-        in_specs=[in_smem, in_vmem, in_vmem],
-        out_specs=(anywhere, anywhere),
+        in_specs=[in_smem, anywhere, anywhere, anywhere],
+        out_specs=(anywhere, anywhere, anywhere),
         scratch_shapes=[
             pltpu.VMEM((span, portion, 128), BF16),
             pltpu.VMEM((span, 2, ranks, head_half), BF16),
+            pltpu.VMEM((all_blocks, portion, 128), BF16),
+            pltpu.VMEM((2, all_blocks, ranks, head_half), BF16),
+            pltpu.VMEM((rows, features), BF16),
             pltpu.VMEM((all_blocks, portion, 128), BF16),
             pltpu.VMEM((all_blocks, 2, ranks, head_half), BF16),
             pltpu.VMEM((portion, 128), F32),
             pltpu.VMEM((2, ranks, head_half), F32),
             pltpu.SMEM((all_blocks,), jnp.int32),
+            dma((2,)),
+            dma((2,)),
             dma((2, total // span)),
             dma((2, all_blocks)),
         ],
-        compiler_params=pltpu.CompilerParams(vmem_limit_bytes=32 * 2**20),
+        compiler_params=pltpu.CompilerParams(vmem_limit_bytes=60 * 2**20),
         name="table",
-    )(adapter_of_block, back_down, back_up)
+    )(adapter_of_block, back_down, back_up, input_gradient)
     down_grad = down_grad.reshape(total, length // 128, 2, 128).transpose(0, 2, 1, 3)
     return (input_gradient, down_grad.reshape(total, 2, length), up_grad)
 

time: 197 us -> 136 us (0.69)
  Pallas kernels: 187 us -> 131 us
  local copies, waits for them, and re-layouts: 6.56 us -> 2.12 us
    pallas_call x1, Pallas kernels: 57.6 us -> 3.71 us  [slice_on_device(): pl.pallas_call(pick_kernel, out_shape=(jax.ShapeDtypeStruct((all_blocks,...]
    pallas_call x1, Pallas kernels: 123 us -> 117 us  [slice_on_device(): pl.pallas_call(layer_kernel, out_shape=(jax.ShapeDtypeStruct((rows, featu...]
    unnamed x8 -> x3, local copies, waits for them, and re-layouts: 5.71 us -> 1.27 us
    pallas_call x1, Pallas kernels: 6.26 us -> 10.4 us  [slice_on_device(): pl.pallas_call(table_kernel, out_shape=(jax.ShapeDtypeStruct((rows, featu...]
where the time goes in v2:
time: 136 us
  Pallas kernels  131 us (96%)
  other arithmetic  2.45 us (2%)
  local copies, waits for them, and re-layouts  2.12 us (2%)
    pallas_call x1, Pallas kernels, slice_on_device(): pl.pallas_call(layer_kernel, out_shape=(jax.ShapeDtypeStruct((rows, featu...  117 us
    pallas_call x1, Pallas kernels, slice_on_device(): pl.pallas_call(table_kernel, out_shape=(jax.ShapeDtypeStruct((rows, featu...  10.4 us
    pallas_call x1, Pallas kernels, slice_on_device(): pl.pallas_call(pick_kernel, out_shape=(jax.ShapeDtypeStruct((all_blocks,...  3.71 us

profile of v2, /device:TPU:0, one launch (start us, length us, event | category | flops | bytes accessed | tf_op | source)
XLA Modules:
  0.0 135.8 jit_solution(14791877397916829939)
XLA Ops:
  0.6 0.0 copy-start
  0.6 0.8 dynamic_slice.3
  1.5 0.1 iota_compare_fusion
  1.6 2.4 %fusion.cot_ref = bf16[2,512,512]{2,1,0:T(8,128)(2,1)} fusion(bf16[512,2,512]{2,1,0:T(2,128)(2,1)} %param.8, pred[512]{0:T(512)(128)(4,1)S(1)} %lt.27), kind=kLoop, calls=%fused_computation.2 | loop fusion | flops 524288 | bytes 2097664 | tf_op jit(solution)/shard_map/transpose | solution.py:547
  3.9 0.0 copy-done
  4.0 1.3 copy.18
  5.2 3.7 %pick.1 = (bf16[16,2,20480]{2,1,0:T(2,128)(2,1)}, bf16[16,2,16,512]{3,2,1,0:T(8,128)(2,1)}) custom-call(s32[16]{0:T(128)} %ids_ref.3, bf16[96,2,20480]{2,1,0:T(2,128)(2,1)} %first_ref.1, bf16[96,2,16,512]{3,2,1,0:T(8,128)(2,1)} %second_ref.1), custom_call_target="tpu_custom_call" | custom-call | tf_op jit(solution)/shard_map/pick/pallas_call | solution.py:550
  8.9 116.5 %layer.1 = (bf16[1024,1280]{1,0:T(8,128)(2,1)}, bf16[16,320,128]{2,1,0:T(8,128)(2,1)}, bf16[2,16,16,512]{3,2,1,0:T(8,128)(2,1)}) custom-call(bf16[2,512,512]{2,1,0:T(8,128)(2,1)} %fusion.cot_ref, bf16[2,640,512]{2,1,0:T(8,128)(2,1)} %bitcast.15, bf16[16,320,128]{2,1,0:T(8,128)(2,1)} %bitcast.16, bf16[16,2,16,512]{3,2,1,0:T(8,128)(2,1)} %get-tuple-element.12.second_ref, ...), custom_call_target="tpu_custom_call" | custom-call | tf_op jit(solution)/shard_map/layer/pallas_call | solution.py:565
  125.5 10.4 %table.1 = (bf16[1024,1280]{1,0:T(8,128)(2,1)}, bf16[96,320,128]{2,1,0:T(8,128)(2,1)}, bf16[96,2,16,512]{3,2,1,0:T(8,128)(2,1)}) custom-call(s32[16]{0:T(128)} %ids_ref.3, bf16[16,320,128]{2,1,0:T(8,128)(2,1)} %get-tuple-element.13.down_in, bf16[2,16,16,512]{3,2,1,0:T(8,128)(2,1)} %get-tuple-element.14.up_in, bf16[1024,1280]{1,0:T(8,128)(2,1)} %get-tuple-element.15.ig_ref), custom_call_target="tpu_custom_call" | custom-call | tf_op jit(solution)/shard_map/table/pallas_call | solution.py:605
  (1 shorter events, 0.0 us)
Async XLA Ops:
  0.6 3.3 %copy-start = (bf16[640,2,512]{2,1,0:T(2,128)(2,1)S(1)}, bf16[640,2,512]{2,1,0:T(2,128)(2,1)}, u32[]{:S(2)}) copy-start(bf16[640,2,512]{2,1,0:T(2,128)(2,1)} %param.9) | copy-start | bytes 3932164

commit v3 on v2

--- a/solution.py
+++ b/solution.py
@@ -239,10 +239,10 @@
     ig_ref, down_ref, up_ref,
     cot, weight, first, first_rows, second, acts,
     head_part, head_got, head, low_part, low_got, low_sum, low,
-    down_stage, up_stage, part, part_got,
+    down_stage, up_stage, part, part_got, ig,
     local_sem, b_send, b_recv, a_send, a_recv, d_send, d_recv, u_send, u_recv,
     c_send, c_recv, h_send, h_recv, l_send, l_recv,
-    w_send, w_recv, y_send, y_recv, p_send, p_recv, x_send, x_recv,
+    w_send, w_recv, y_send, y_recv, p_send, p_recv, x_send, x_recv, ig_sem,
 ):
     f = lax.axis_index("fsdp")
     g = lax.axis_index("groups")
@@ -480,12 +480,16 @@
         part_copy(2 * t + h, h).wait_recv()
     width = part.shape[2]
 
+    def ig_copy(b):
+        return pltpu.make_async_copy(ig.at[columns(b)], ig_ref.at[columns(b)], ig_sem.at[b])
+
     def final_block(b, carry):
         grad = head_of(b).astype(F32).T.astype(BF16)
         for h in range(2):
             term = product(grad, first_rows[b, pl.ds(h * width, width)], 1, 1)
             base = part[2 * t + h, columns(b)].astype(F32) + part_got[h, columns(b)].astype(F32)
-            ig_ref[columns(b), pl.ds(h * width, width)] = (base + adapter_scale * term).astype(BF16)
+            ig[columns(b), pl.ds(h * width, width)] = (base + adapter_scale * term).astype(BF16)
+        ig_copy(b).start()
         return carry
 
     lax.fori_loop(0, blocks, final_block, 0)
@@ -501,6 +505,8 @@
         part_copy(2 * other_t + h, h).wait_send()
     for copy in pending:
         copy.wait_send()
+    for b in range(blocks):
+        ig_copy(b).wait()
 
     @pl.when(inner)
     def _():
@@ -570,7 +576,7 @@
             jax.ShapeDtypeStruct((2, all_blocks, ranks, head_half), BF16),
         ),
         in_specs=[anywhere] * 5,
-        out_specs=(in_vmem, anywhere, anywhere),
+        out_specs=(anywhere, anywhere, anywhere),
         scratch_shapes=[
             pltpu.VMEM((2, rows, head_half), BF16),
             pltpu.VMEM((4, 2, shard, head_half), BF16),
@@ -589,12 +595,13 @@
             pltpu.VMEM((blocks, ADAPTER_RANK, head_half), BF16),
             pltpu.VMEM((4, rows, shard), BF16),
             pltpu.VMEM((2, rows, shard), BF16),
+            pltpu.VMEM((rows, features), BF16),
             dma((7,)),
             dma((3,)), dma((4,)), dma((3,)), dma((4,)),
             dma((3,)), dma((4,)), dma((3,)), dma((4,)),
             dma((2,)), dma((2,)), dma((2,)), dma((2,)), dma((2,)), dma((2,)),
             dma((5, 2)), dma((4, 2)), dma((3, 2)), dma((4, 2)),
-            dma((2,)), dma((2,)), dma((1,)), dma((1,)),
+            dma((2,)), dma((2,)), dma((1,)), dma((1,)), dma((blocks,)),
         ],
         compiler_params=pltpu.CompilerParams(
             collective_id=0, has_side_effects=True, vmem_limit_bytes=58 * 2**20

time: 136 us -> 135 us (level)
  no operation moved by 1% of the time
where the time goes in v3:
time: 135 us
  Pallas kernels  130 us (96%)
  other arithmetic  2.45 us (2%)
  local copies, waits for them, and re-layouts  2.12 us (2%)
    pallas_call x1, Pallas kernels, slice_on_device(): pl.pallas_call(layer_kernel, out_shape=(jax.ShapeDtypeStruct((rows, featu...  115 us
    pallas_call x1, Pallas kernels, slice_on_device(): pl.pallas_call(table_kernel, out_shape=(jax.ShapeDtypeStruct((rows, featu...  10.8 us
    pallas_call x1, Pallas kernels, slice_on_device(): pl.pallas_call(pick_kernel, out_shape=(jax.ShapeDtypeStruct((all_blocks,...  3.71 us

profile of v3, /device:TPU:0, one launch (start us, length us, event | category | flops | bytes accessed | tf_op | source)
XLA Modules:
  0.0 135.0 jit_solution(1302232458043927134)
XLA Ops:
  0.6 0.0 copy-start
  0.6 0.8 dynamic_slice.3
  1.5 0.1 iota_compare_fusion
  1.6 2.4 %fusion.cot_ref = bf16[2,512,512]{2,1,0:T(8,128)(2,1)} fusion(bf16[512,2,512]{2,1,0:T(2,128)(2,1)} %param.8, pred[512]{0:T(512)(128)(4,1)S(1)} %lt.27), kind=kLoop, calls=%fused_computation.2 | loop fusion | flops 524288 | bytes 2097664 | tf_op jit(solution)/shard_map/transpose | solution.py:553
  3.9 0.0 copy-done
  4.0 1.3 copy.18
  5.2 3.7 %pick.1 = (bf16[16,2,20480]{2,1,0:T(2,128)(2,1)}, bf16[16,2,16,512]{3,2,1,0:T(8,128)(2,1)}) custom-call(s32[16]{0:T(128)} %ids_ref.3, bf16[96,2,20480]{2,1,0:T(2,128)(2,1)} %first_ref.1, bf16[96,2,16,512]{3,2,1,0:T(8,128)(2,1)} %second_ref.1), custom_call_target="tpu_custom_call" | custom-call | tf_op jit(solution)/shard_map/pick/pallas_call | solution.py:556
  8.9 115.3 %layer.1 = (bf16[1024,1280]{1,0:T(8,128)(2,1)}, bf16[16,320,128]{2,1,0:T(8,128)(2,1)}, bf16[2,16,16,512]{3,2,1,0:T(8,128)(2,1)}) custom-call(bf16[2,512,512]{2,1,0:T(8,128)(2,1)} %fusion.cot_ref, bf16[2,640,512]{2,1,0:T(8,128)(2,1)} %bitcast.15, bf16[16,320,128]{2,1,0:T(8,128)(2,1)} %bitcast.16, bf16[16,2,16,512]{3,2,1,0:T(8,128)(2,1)} %get-tuple-element.12.second_ref, ...), custom_call_target="tpu_custom_call" | custom-call | tf_op jit(solution)/shard_map/layer/pallas_call | solution.py:571
  124.2 10.8 %table.1 = (bf16[1024,1280]{1,0:T(8,128)(2,1)}, bf16[96,320,128]{2,1,0:T(8,128)(2,1)}, bf16[96,2,16,512]{3,2,1,0:T(8,128)(2,1)}) custom-call(s32[16]{0:T(128)} %ids_ref.3, bf16[16,320,128]{2,1,0:T(8,128)(2,1)} %get-tuple-element.13.down_in, bf16[2,16,16,512]{3,2,1,0:T(8,128)(2,1)} %get-tuple-element.14.up_in, bf16[1024,1280]{1,0:T(8,128)(2,1)} %get-tuple-element.15.ig_ref), custom_call_target="tpu_custom_call" | custom-call | tf_op jit(solution)/shard_map/table/pallas_call | solution.py:612
  (1 shorter events, 0.0 us)
Async XLA Ops:
  0.6 3.3 %copy-start = (bf16[640,2,512]{2,1,0:T(2,128)(2,1)S(1)}, bf16[640,2,512]{2,1,0:T(2,128)(2,1)}, u32[]{:S(2)}) copy-start(bf16[640,2,512]{2,1,0:T(2,128)(2,1)} %param.9) | copy-start | bytes 3932164
